TPU v7x, 512 devices: a whole 4x4x16 slice. The times are simulated.
512 devices in a mesh: replica: 8 (over z_lo, core), fsdp: 64 (over x, y, z_hi).
Axes of the slice: x: 4, y: 4, z: 16 (z_hi: 4, z_lo: 4; z = z_hi * 4 + z_lo), core: 2. Of those that a mesh axis runs over, the one named last changes fastest.
Arguments:
- activations: bfloat16 [8, 8192, 4096], P('replica', 'fsdp'), may hold values from -6 to 6
- cotangent: bfloat16 [8, 8192, 512], P('replica', 'fsdp'), may hold values from -6 to 6
- weights: bfloat16 [8, 4096, 512], P('replica', 'fsdp'), may hold values from -0.09375 to 0.09375
- stale_params: bfloat16 [8, 4, 4096, 512], P('replica', None, 'fsdp'), may hold values from -0.09375 to 0.09375
- global_params: float32 [4, 4096, 512], P(None, 'fsdp'), may hold values from -0.09375 to 0.09375
- momentum: float32 [4, 4096, 512], P(None, 'fsdp'), may hold values from -0.3125 to 0.3125
- plan: int32 [1], replicated, may hold values from 0 to 999
Outputs:
- values_out: bfloat16 [8, 8192, 512], P('replica', 'fsdp')
- input_grad: bfloat16 [8, 8192, 4096], P('replica', 'fsdp')
- new_weights: bfloat16 [8, 4096, 512], P('replica', 'fsdp')
- new_global: float32 [4, 4096, 512], P(None, 'fsdp')
- new_momentum: float32 [4, 4096, 512], P(None, 'fsdp')
All inputs are finite; a program needn't handle non-finite values.
Results may differ from a plain program's by a relative error of at most 0.001.
Values may be sent and summed in bfloat16 or wider, within the bound.
A program may use at most 64 MiB of HBM per device.

v0:
```python
import jax
import jax.numpy as jnp
from jax import lax
from jax.sharding import PartitionSpec as P


def per_device(activations, cotangent, weights, stale_params, global_params, momentum, plan):
    inputs = activations[0]
    grads = cotangent[0]
    weight = weights[0]
    full_weight = lax.all_gather(weight, "fsdp", axis=0, tiled=True)
    values_out = jnp.dot(inputs, full_weight, preferred_element_type=jnp.float32).astype(
        jnp.bfloat16
    )
    input_grad = jnp.dot(grads, full_weight.T, preferred_element_type=jnp.float32).astype(
        jnp.bfloat16
    )
    columns = lax.all_to_all(inputs, "fsdp", split_axis=1, concat_axis=0, tiled=True)
    all_grads = lax.all_gather(grads, "fsdp", axis=0, tiled=True)
    weight_grad = jnp.dot(columns.T, all_grads, preferred_element_type=jnp.float32)
    inner = weight.astype(jnp.float32) - 0.0002 * weight_grad
    frag_count = global_params.shape[0]
    frag = plan[0] % frag_count
    picked = jnp.arange(frag_count, dtype=jnp.int32) == frag
    global_old = jnp.sum(jnp.where(picked[:, None, None], global_params, 0.0), axis=0)
    moment_old = jnp.sum(jnp.where(picked[:, None, None], momentum, 0.0), axis=0)
    stale = jnp.sum(
        jnp.where(picked[:, None, None], stale_params[0].astype(jnp.float32), 0.0), axis=0
    )
    delta = global_old - stale
    replicas = lax.axis_size("replica")
    mean_delta = lax.psum(delta, "replica") / replicas
    moment_f = 0.9 * moment_old + mean_delta
    global_f = global_old - 0.7 * (mean_delta + 0.9 * moment_f)
    new_global = jnp.where(picked[:, None, None], global_f[None], global_params)
    new_momentum = jnp.where(picked[:, None, None], moment_f[None], momentum)
    mixed = (0.5 * inner + 0.5 * global_f).astype(jnp.bfloat16)
    return (values_out[None], input_grad[None], mixed[None], new_global, new_momentum)


def solution(mesh):
    placed = (
        P("replica", "fsdp", None),
        P("replica", "fsdp", None),
        P("replica", "fsdp", None),
        P("replica", None, "fsdp", None),
        P(None, "fsdp", None),
        P(None, "fsdp", None),
        P(),
    )
    return jax.shard_map(
        per_device,
        mesh=mesh,
        in_specs=placed,
        out_specs=(
            P("replica", "fsdp", None),
            P("replica", "fsdp", None),
            P("replica", "fsdp", None),
            P(None, "fsdp", None),
            P(None, "fsdp", None),
        ),
        check_vma=False,
    )
```

profile of v0, /device:TPU:1, one launch (start us, length us, event | category | flops | bytes accessed | tf_op | source)
XLA Modules:
  0.0 387.1 jit_solution(3220616593416180434)
XLA Ops:
  8.0 0.0 copy-start.3
  8.0 0.0 copy-start.2
  8.0 0.0 all-reduce.2.cloned.1.call-start
  8.8 1.5 select_reduce_fusion
  10.3 0.7 sub.10
  11.0 0.0 all-reduce.2.cloned.1.call-update
  11.0 0.0 all-gather.5.cloned.1.call-start
  11.1 0.5 all-gather.5.cloned.1.call-update
  11.6 0.0 all-gather.7.cloned.1.call-start
  11.7 0.5 all-gather.7.cloned.1.call-update
  12.2 2.3 copy.12
  14.5 21.7 %all-to-all-start = ((bf16[128,64,64]{0,2,1:T(8,128)(2,1)}), bf16[128,64,64]{0,2,1:T(8,128)(2,1)S(1)}, u32[]{:S(2)}, u32[]{:S(2)}) async-start(bf16[128,64,64]{0,2,1:T(8,128)(2,1)} %bitcast.6), calls=%async_computation | async-start | bytes 2097152 | tf_op jit(solution)/shard_map/all_to_all | solution.py:18
  36.3 89.7 %all-reduce.2.cloned.1.call-done = f32[64,512]{1,0:T(8,128)} async-done(((f32[64,512]{1,0:T(8,128)}), f32[64,512]{1,0:T(8,128)}) %all-reduce.2.cloned.1.call-update) | async-done | bytes 131088 | tf_op jit(solution)/shard_map/psum | solution.py:32
  125.9 0.0 copy-start.1
  125.9 1.0 multiply_add_fusion
  127.0 0.0 copy-done.3
  127.0 0.0 copy-done.2
  127.0 1.2 broadcast_select_fusion
  128.2 0.0 copy-start.4
  128.2 51.4 %all-gather.5.cloned.1.call-done = bf16[1,4096,512]{2,1,0:T(8,128)(2,1)} async-done(((bf16[1,64,512]{2,1,0:T(8,128)(2,1)}), bf16[1,4096,512]{2,1,0:T(8,128)(2,1)}) %all-gather.5.cloned.1.call-update) | async-done | bytes 4194320 | tf_op jit(solution)/shard_map/all_gather | solution.py:11
  179.5 0.0 copy-start
  179.5 4.8 %fusion.2 = bf16[1,128,4096]{2,1,0:T(8,128)(2,1)} fusion(bf16[1,4096,512]{2,1,0:T(8,128)(2,1)} %all-gather.5.cloned.1.call-done, bf16[1,128,512]{2,1,0:T(8,128)(2,1)} %param.8), kind=kOutput, calls=%fused_computation.3 | convolution fusion | flops 537395200 | bytes 5373952 | tf_op jit(solution)/shard_map/dot_general | solution.py:15
  184.4 0.0 copy-done.1
  184.4 0.0 copy-done
  184.4 1.4 fusion.9
  185.8 0.0 all-to-all-done
  185.8 188.3 %all-gather.7.cloned.1.call-done = bf16[1,8192,512]{2,1,0:T(8,128)(2,1)} async-done(((bf16[1,128,512]{2,1,0:T(8,128)(2,1)}), bf16[1,8192,512]{2,1,0:T(8,128)(2,1)}) %all-gather.7.cloned.1.call-update) | async-done | bytes 8388624 | tf_op jit(solution)/shard_map/all_gather | solution.py:19
  374.1 0.0 copy-done.4
  374.1 5.6 %fusion.27 = bf16[1,64,512]{2,1,0:T(8,128)(2,1)} fusion(f32[64,512]{1,0:T(8,128)S(1)} %get-tuple-element.9, bf16[1,8192,512]{2,1,0:T(8,128)(2,1)} %all-gather.7.cloned.1.call-done, bf16[1,64,512]{2,1,0:T(8,128)(2,1)S(1)} %copy-done.4, bf16[128,64,64]{0,2,1:T(8,128)(2,1)S(1)} %all-to-all-done), kind=kOutput, calls=%fused_computation.14 | convolution fusion | flops 537067520 | bytes 9699328 | tf_op jit(solution)/shard_map/dot_general | solution.py:20
  (1 shorter events, 0.0 us)
Async XLA Ops:
  8.0 119.0 %copy-start.3 = (f32[4,64,512]{2,1,0:T(8,128)S(1)}, f32[4,64,512]{2,1,0:T(8,128)}, u32[]{:S(2)}) copy-start(f32[4,64,512]{2,1,0:T(8,128)} %param.11) | copy-start | bytes 1572868
  8.0 119.0 %copy-start.2 = (f32[4,64,512]{2,1,0:T(8,128)S(1)}, f32[4,64,512]{2,1,0:T(8,128)}, u32[]{:S(2)}) copy-start(f32[4,64,512]{2,1,0:T(8,128)} %param.12) | copy-start | bytes 1572868
  8.0 117.9 %all-reduce.2.cloned.1.call-start = ((), (), s32[]{:S(2)}) async-start(), calls=%async_computation.1 | async-start | bytes 262144 | tf_op jit(solution)/shard_map/psum | solution.py:32
  11.0 168.5 %all-gather.5.cloned.1.call-start = ((), (), s32[]{:S(2)}) async-start(), calls=%async_computation.2 | async-start | bytes 4259840 | tf_op jit(solution)/shard_map/all_gather | solution.py:11
  11.6 362.5 %all-gather.7.cloned.1.call-start = ((), (), s32[]{:S(2)}) async-start(), calls=%async_computation.3 | async-start | bytes 8519680 | tf_op jit(solution)/shard_map/all_gather | solution.py:19
  14.5 171.3 %all-to-all-start = ((bf16[128,64,64]{0,2,1:T(8,128)(2,1)}), bf16[128,64,64]{0,2,1:T(8,128)(2,1)S(1)}, u32[]{:S(2)}, u32[]{:S(2)}) async-start(bf16[128,64,64]{0,2,1:T(8,128)(2,1)} %bitcast.6), calls=%async_computation | async-start | bytes 2097152 | tf_op jit(solution)/shard_map/all_to_all | solution.py:18
  125.9 58.5 %copy-start.1 = (bf16[1,128,4096]{2,1,0:T(8,128)(2,1)S(1)}, bf16[1,128,4096]{2,1,0:T(8,128)(2,1)}, u32[]{:S(2)}) copy-start(bf16[1,128,4096]{2,1,0:T(8,128)(2,1)} %param.7) | copy-start | bytes 3145732
  128.2 245.9 %copy-start.4 = (bf16[1,64,512]{2,1,0:T(8,128)(2,1)S(1)}, bf16[1,64,512]{2,1,0:T(8,128)(2,1)}, u32[]{:S(2)}) copy-start(bf16[1,64,512]{2,1,0:T(8,128)(2,1)} %param.9) | copy-start | bytes 196612
  179.5 4.9 %copy-start = (bf16[1,4096,512]{2,1,0:T(8,128)(2,1)S(1)}, bf16[1,4096,512]{2,1,0:T(8,128)(2,1)}, u32[]{:S(2)}) copy-start(bf16[1,4096,512]{2,1,0:T(8,128)(2,1)} %all-gather.5.cloned.1.call-done) | copy-start | bytes 12582916
Sparse Core Ops, SparseCore 0:
  12.3 113.5 all-reduce.1
Sparse Core Ops, SparseCore 1:
  15.7 163.8 all-gather.4
  184.3 189.7 all-gather.6
where the time goes:
time: 387 us
  waiting for transfers between devices  330 us (85%)
  starting transfers between devices  21.9 us (6%)
  between operations  16.3 us (4%)
  matrix products  11.8 us (3%)
  other arithmetic  4.42 us (1%)
    all_gather x1, waiting for transfers between devices, per_device(): all_grads = lax.all_gather(grads, 'fsdp', axis=0, tiled=True)  188 us
    psum x1, waiting for transfers between devices, per_device(): mean_delta = lax.psum(delta, 'replica') / replicas  89.7 us
    all_gather x1, waiting for transfers between devices, per_device(): full_weight = lax.all_gather(weight, 'fsdp', axis=0, tiled=True)  51.4 us
    all_to_all x1, starting transfers between devices, per_device(): lax.all_to_all(inputs, 'fsdp', split_axis=1, concat_axis=0, tiled=True)  21.7 us
  transfers between devices with their start and end apart: 4, of which 3 were waited for; matrix products, arithmetic and copies ran while one was open for 3% of the time, Pallas kernels for 0%

commit v1 on v0

v1 whole, which is shorter than its diff:
```python
import functools

import jax
import jax.numpy as jnp
from jax import lax
from jax.experimental import pallas as pl
from jax.experimental.pallas import tpu as pltpu
from jax.sharding import PartitionSpec as P

MESH = pl.DeviceIdType.MESH
F32 = jnp.float32
BF16 = jnp.bfloat16
T = 128
F = 512
B = 64
RATE = 0.0002


def kernel(
    plan_ref, act_ref, cot_ref, w_ref, stale_ref, glob_ref, mom_ref,
    values_ref, igrad_ref, neww_ref, newg_ref, newm_ref,
    actg, cotg, wg, dwp, yrs, zsum, zrs, vp, vrs, ig, vout, wout,
    stl, sel, selp, chip, rsr, sg, gin, minn, gout, mout,
    s_cot, r_cot, s_act, r_act, s_wz, r_wz, s_wy, r_wy, s_y, r_y, s_z, r_z,
    s_ig, r_ig, s_v, r_v, s_st, r_st, l_in, l_act, l_out,
):
    rep = lax.axis_index("replica")
    fs = lax.axis_index("fsdp")
    zl, core = rep // 2, rep % 2
    x, y, z = fs // 16, (fs // 4) % 4, fs % 4
    zz = z % 2
    pair = z // 2

    def at_x(d):
        return (rep, ((x + d) % 4) * 16 + y * 4 + z)

    def at_y(d):
        return (rep, x * 16 + ((y + d) % 4) * 4 + z)

    z_of = (z + 1 - 2 * zz, 3 - z, (z + 2) % 4)

    def at_z(k):
        return (rep, x * 16 + y * 4 + z_of[k])

    def at_zl(d):
        return (((zl + d) % 4) * 2 + core, fs)

    other_core = (zl * 2 + 1 - core, fs)

    def rdma(src, dst, send, recv, to):
        return pltpu.make_async_remote_copy(
            src_ref=src, dst_ref=dst, send_sem=send, recv_sem=recv, device_id=to, device_id_type=MESH
        )

    def rows(i, n):
        return pl.ds(pl.multiple_of(i * n, n), n)

    def channels(xx, yy, half):
        zp = half * pair + (1 - half) * (1 - pair)
        return pl.ds(pl.multiple_of(xx * 1024 + yy * 256 + zp * 128, 128), 128)

    loads = [
        pltpu.make_async_copy(stale_ref, stl, l_in.at[0]),
        pltpu.make_async_copy(glob_ref, gin, l_in.at[1]),
        pltpu.make_async_copy(mom_ref, minn, l_in.at[2]),
        pltpu.make_async_copy(cot_ref, cotg.at[rows(x, T)], l_in.at[3]),
        pltpu.make_async_copy(w_ref, wg.at[1, pl.ds(pl.multiple_of(y * 128 + zz * 64, 64), B)], l_in.at[4]),
    ]
    for c in loads:
        c.start()
    for half in (0, 1):
        for yy in range(4):
            pltpu.make_async_copy(
                act_ref.at[:, channels(x, yy, half)], actg.at[half, rows(x, T), pl.ds(yy * 128, 128)], l_act.at[half]
            ).start()

    barrier = pltpu.get_barrier_semaphore()
    greet = [at_x(d) for d in (1, 2, 3)] + [at_y(d) for d in (1, 2, 3)] + [at_z(k) for k in range(3)]
    greet += [at_zl(d) for d in (1, 2, 3)] + [other_core]
    for to in greet:
        pl.semaphore_signal(barrier, inc=1, device_id=to, device_id_type=MESH)
    pl.semaphore_wait(barrier, len(greet))

    ORDER = (1, 3, 2)
    cots = [rdma(cot_ref, cotg.at[rows(x, T)], s_cot.at[d - 1], r_cot.at[d - 1], at_x(d)) for d in (1, 2, 3)]
    for d in ORDER:
        cots[d - 1].start()

    def w_rows(zpar):
        return pl.ds(pl.multiple_of(y * 128 + zpar * 64, 64), B)

    wz = [
        rdma(w_ref, wg.at[1 if k == 0 else 0, w_rows(zz)], s_wz.at[k], r_wz.at[k], at_z(k)) for k in range(3)
    ]
    for k in range(3):
        wz[k].start()
    slots = ((1, zz), (1, 1 - zz), (0, 1 - zz), (0, zz))

    def wy(slot, d):
        half, zpar = slots[slot]
        there = wg.at[half, w_rows(zpar)]
        return rdma(w_ref if slot == 0 else there, there, s_wy.at[slot, d - 1], r_wy.at[slot, d - 1], at_y(d))

    for d in ORDER:
        wy(0, d).start()

    def act_send(half, yy, d):
        return rdma(
            act_ref.at[:, channels((x + d) % 4, yy, half)],
            actg.at[half, rows(x, T), pl.ds(yy * 128, 128)],
            s_act.at[half, d - 1],
            r_act.at[half, d - 1],
            at_x(d),
        )

    for half in (0, 1):
        for yy in range(4):
            for d in ORDER:
                act_send(half, yy, d).start()

    def act_all(half, d):
        there = actg.at[half, rows(x, T)]
        return rdma(there, there, s_act.at[half, d - 1], r_act.at[half, d - 1], at_x(d))

    frag = plan_ref[0] % 4
    loads[0].wait()
    picked = jnp.zeros((B, F), F32)
    for k in range(4):
        picked = jnp.where(frag == k, stl[k].astype(F32), picked)
    sel[...] = picked.astype(BF16)
    to_core = rdma(sel, selp, s_st.at[0], r_st.at[0], other_core)
    to_core.start()
    to_core.wait_recv()
    chip[...] = (sel[...].astype(F32) + selp[...].astype(F32)).reshape(4, 2, 8, F)
    scatter = [
        rdma(chip.at[(zl + d) % 4, core], rsr.at[d - 1], s_st.at[d], r_st.at[d], at_zl(d)) for d in (1, 2, 3)
    ]
    for c in scatter:
        c.start()

    def pass_on(k):
        wz[k].wait_recv()
        for d in ORDER:
            wy(k + 1, d).start()

    pass_on(0)

    for c in scatter:
        c.wait_recv()
    sg[zl, core] = chip[zl, core] + rsr[0] + rsr[1] + rsr[2]
    spread = [
        rdma(sg.at[zl, core], sg.at[zl, core], s_st.at[3 + d], r_st.at[3 + d], at_zl(d)) for d in (1, 2, 3)
    ]
    for c in spread:
        c.start()

    pass_on(1)
    loads[3].wait()
    for c in cots:
        c.wait_recv()

    def y_send(half, zpar, d):
        to = (y + d) % 4
        return rdma(
            dwp.at[half, pl.ds(pl.multiple_of(to * 128 + zpar * 64, 64), B)],
            yrs.at[half, zpar, d - 1],
            s_y.at[half, zpar, d - 1],
            r_y.at[half, zpar, d - 1],
            at_y(d),
        )

    def weight_grad(half, first):
        whole = actg.at[half, rows(x, T)]
        pltpu.make_async_copy(whole, whole, l_act.at[half]).wait()
        for d in ORDER:
            act_all(half, d).wait_recv()

        def step(i, carry):
            yy = (y + 2 + i) % 4
            cols = pl.ds(pl.multiple_of(yy * 128, 128), 128)
            dwp[half, cols] = lax.dot_general(
                actg[half, :, cols], cotg[...], (((0,), (0,)), ((), ())), preferred_element_type=F32
            )
            return carry

        lax.fori_loop(0, 4, step, 0)
        for zpar in (first, 1 - first):
            for d in ORDER:
                y_send(half, zpar, d).start()

    weight_grad(0, zz)

    def ig_send(half, yy, d):
        return rdma(
            ig.at[half, rows((x + d) % 4, T), pl.ds(yy * 128, 128)],
            igrad_ref.at[:, channels(x, yy, half)],
            s_ig.at[half, d - 1],
            r_ig.at[half, d - 1],
            at_x(d),
        )

    def input_grad(half):
        def step(i, carry):
            block = rows((x + 2 + i) % 4, T)
            ig[half, block] = lax.dot_general(
                cotg[block], wg[half], (((1,), (1,)), ((), ())), preferred_element_type=F32
            ).astype(BF16)
            return carry

        lax.fori_loop(0, 4, step, 0)
        for yy in range(4):
            for d in ORDER:
                ig_send(half, yy, d).start()
            pltpu.make_async_copy(
                ig.at[half, rows(x, T), pl.ds(yy * 128, 128)], igrad_ref.at[:, channels(x, yy, half)], l_out.at[half]
            ).start()

    loads[4].wait()
    for slot in (0, 1):
        for d in ORDER:
            wy(slot, d).wait_recv()
    input_grad(1)

    pass_on(2)
    weight_grad(1, 1 - zz)

    def z_send(k):
        return rdma(zsum.at[k], zrs.at[k], s_z.at[k], r_z.at[k], at_z(k))

    def over_y(half, zpar):
        for d in ORDER:
            y_send(half, zpar, d).wait_recv()
        mine = dwp[half, pl.ds(pl.multiple_of(y * 128 + zpar * 64, 64), B)]
        return mine + yrs[half, zpar, 0] + yrs[half, zpar, 1] + yrs[half, zpar, 2]

    zsum[2] = over_y(0, zz)
    z_send(2).start()

    for slot in (2, 3):
        for d in ORDER:
            wy(slot, d).wait_recv()
    input_grad(0)

    def values_step(i, carry):
        block = rows((x + 1 + i) % 4, T)
        vp[block] = jnp.dot(actg[0, block], wg[0], preferred_element_type=F32) + jnp.dot(
            actg[1, block], wg[1], preferred_element_type=F32
        )
        return carry

    lax.fori_loop(0, 4, values_step, 0)

    def v_send(d):
        return rdma(vp.at[rows((x + d) % 4, T)], vrs.at[d - 1], s_v.at[d - 1], r_v.at[d - 1], at_x(d))

    for d in ORDER:
        v_send(d).start()

    zsum[1] = over_y(0, 1 - zz)
    z_send(1).start()
    zsum[0] = over_y(1, 1 - zz)
    z_send(0).start()

    for c in spread:
        c.wait_recv()
    across = rdma(sg.at[:, core], sg.at[:, core], s_st.at[7], r_st.at[7], other_core)
    across.start()
    across.wait_recv()
    loads[1].wait()
    loads[2].wait()
    old = jnp.zeros((B, F), F32)
    moment = jnp.zeros((B, F), F32)
    for k in range(4):
        old = jnp.where(frag == k, gin[k], old)
        moment = jnp.where(frag == k, minn[k], moment)
    mean = old - sg[...].reshape(B, F) / 8.0
    moment = 0.9 * moment + mean
    new = old - 0.7 * (mean + 0.9 * moment)
    for k in range(4):
        gout[k] = jnp.where(frag == k, new, gin[k])
        mout[k] = jnp.where(frag == k, moment, minn[k])
    stores = [
        pltpu.make_async_copy(gout, newg_ref, l_out.at[2]),
        pltpu.make_async_copy(mout, newm_ref, l_out.at[3]),
    ]
    stores[0].start()
    stores[1].start()

    zsum[3] = over_y(1, zz)

    for d in ORDER:
        v_send(d).wait_recv()
    vout[...] = (vp[rows(x, T)] + vrs[0] + vrs[1] + vrs[2]).astype(BF16)
    stores.append(pltpu.make_async_copy(vout, values_ref, l_out.at[4]))
    stores[2].start()

    for k in range(3):
        z_send(k).wait_recv()
    grad = zsum[3] + zrs[0] + zrs[1] + zrs[2]
    inner = wg[1, w_rows(zz)].astype(F32) - RATE * grad
    picked = jnp.zeros((B, F), F32)
    for k in range(4):
        picked = jnp.where(frag == k, gout[k], picked)
    wout[...] = (0.5 * inner + 0.5 * picked).astype(BF16)
    stores.append(pltpu.make_async_copy(wout, neww_ref, l_out.at[5]))
    stores[3].start()

    for half in (0, 1):
        landed = igrad_ref.at[:, pl.ds(0, 512)]
        for d in (1, 2, 3):
            own = ig.at[half, rows((x + d) % 4, T)]
            back = rdma(own, landed, s_ig.at[half, d - 1], r_ig.at[half, d - 1], at_x(d))
            back.wait_recv()
            back.wait_send()
            act_all(half, d).wait_send()
        pltpu.make_async_copy(ig.at[half, rows(x, T)], landed, l_out.at[half]).wait()
    for c in cots + wz + scatter + spread + [to_core, across]:
        c.wait_send()
    for d in (1, 2, 3):
        v_send(d).wait_send()
        for slot in range(4):
            wy(slot, d).wait_send()
        for half in (0, 1):
            for zpar in (0, 1):
                y_send(half, zpar, d).wait_send()
    for k in range(3):
        z_send(k).wait_send()
    for c in stores:
        c.wait()


def per_device(activations, cotangent, weights, stale_params, global_params, momentum, plan):
    anywhere = pl.BlockSpec(memory_space=pl.ANY)
    dma = pltpu.SemaphoreType.DMA
    outs = pl.pallas_call(
        kernel,
        name="diloco_step",
        out_shape=(
            jax.ShapeDtypeStruct((T, F), BF16),
            jax.ShapeDtypeStruct((T, 4096), BF16),
            jax.ShapeDtypeStruct((B, F), BF16),
            jax.ShapeDtypeStruct((4, B, F), F32),
            jax.ShapeDtypeStruct((4, B, F), F32),
        ),
        in_specs=[pl.BlockSpec(memory_space=pltpu.SMEM)] + [anywhere] * 6,
        out_specs=(anywhere,) * 5,
        scratch_shapes=[
            pltpu.VMEM((2, 512, 512), BF16),
            pltpu.VMEM((512, F), BF16),
            pltpu.VMEM((2, 512, F), BF16),
            pltpu.VMEM((2, 512, F), F32),
            pltpu.VMEM((2, 2, 3, B, F), F32),
            pltpu.VMEM((4, B, F), F32),
            pltpu.VMEM((3, B, F), F32),
            pltpu.VMEM((512, F), F32),
            pltpu.VMEM((3, T, F), F32),
            pltpu.VMEM((2, 512, 512), BF16),
            pltpu.VMEM((T, F), BF16),
            pltpu.VMEM((B, F), BF16),
            pltpu.VMEM((4, B, F), BF16),
            pltpu.VMEM((B, F), BF16),
            pltpu.VMEM((B, F), BF16),
            pltpu.VMEM((4, 2, 8, F), F32),
            pltpu.VMEM((3, 8, F), F32),
            pltpu.VMEM((4, 2, 8, F), F32),
            pltpu.VMEM((4, B, F), F32),
            pltpu.VMEM((4, B, F), F32),
            pltpu.VMEM((4, B, F), F32),
            pltpu.VMEM((4, B, F), F32),
            dma((3,)), dma((3,)),
            dma((2, 3)), dma((2, 3)),
            dma((3,)), dma((3,)),
            dma((4, 3)), dma((4, 3)),
            dma((2, 2, 3)), dma((2, 2, 3)),
            dma((3,)), dma((3,)),
            dma((2, 3)), dma((2, 3)),
            dma((3,)), dma((3,)),
            dma((8,)), dma((8,)),
            dma((5,)), dma((2,)), dma((6,)),
        ],
        compiler_params=pltpu.CompilerParams(
            collective_id=0, has_side_effects=True, vmem_limit_bytes=40 << 20
        ),
        cost_estimate=pl.CostEstimate(flops=1_700_000_000, bytes_accessed=7 << 20, transcendentals=0),
    )(plan, activations[0], cotangent[0], weights[0], stale_params[0], global_params, momentum)
    values, igrad, neww, newg, newm = outs
    return (values[None], igrad[None], neww[None], newg, newm)


def solution(mesh):
    placed = (
        P("replica", "fsdp", None),
        P("replica", "fsdp", None),
        P("replica", "fsdp", None),
        P("replica", None, "fsdp", None),
        P(None, "fsdp", None),
        P(None, "fsdp", None),
        P(),
    )
    return jax.shard_map(
        per_device,
        mesh=mesh,
        in_specs=placed,
        out_specs=(
            P("replica", "fsdp", None),
            P("replica", "fsdp", None),
            P("replica", "fsdp", None),
            P(None, "fsdp", None),
            P(None, "fsdp", None),
        ),
        check_vma=False,
    )
```

time: 387 us -> 80.8 us (0.21)
  the two profiles are of different devices: /device:TPU:1 before, /device:TPU:32 now
where the time goes in v1:
time: 80.8 us; the launch traced here: 80.4 us
  Pallas kernels  69.3 us (86%)
  local copies, waits for them, and re-layouts  9.83 us (12%)
  between operations  1.3 us (2%)
    pallas_call x1, Pallas kernels, per_device(): pl.pallas_call(kernel, name='diloco_step', out_shape=(jax.ShapeDtypeStruc...  69.3 us
    unnamed x17, local copies, waits for them, and re-layouts  9.83 us

profile of v1, /device:TPU:32, one launch (start us, length us, event | category | flops | bytes accessed | tf_op | source)
XLA Modules:
  0.0 80.4 jit_solution(1571240260088074739)
XLA Ops:
  1.3 0.0 copy-start
  1.3 1.2 %copy-done = bf16[1,128,4096]{2,1,0:T(8,128)(2,1)S(1)} copy-done((bf16[1,128,4096]{2,1,0:T(8,128)(2,1)S(1)}, bf16[1,128,4096]{2,1,0:T(8,128)(2,1)}, u32[]{:S(2)}) %copy-start) | copy-done | bytes 1048600
  2.5 0.0 copy-start.1
  2.5 1.0 %copy-done.1 = f32[4,64,512]{2,1,0:T(8,128)S(1)} copy-done((f32[4,64,512]{2,1,0:T(8,128)S(1)}, f32[4,64,512]{2,1,0:T(8,128)}, u32[]{:S(2)}) %copy-start.1) | copy-done | bytes 524312
  3.5 0.0 copy-start.2
  3.5 1.0 %copy-done.2 = f32[4,64,512]{2,1,0:T(8,128)S(1)} copy-done((f32[4,64,512]{2,1,0:T(8,128)S(1)}, f32[4,64,512]{2,1,0:T(8,128)}, u32[]{:S(2)}) %copy-start.2) | copy-done | bytes 524312
  4.6 0.0 copy-start.3
  4.6 0.9 %copy-done.3 = bf16[1,4,64,512]{3,2,1,0:T(8,128)(2,1)S(1)} copy-done((bf16[1,4,64,512]{3,2,1,0:T(8,128)(2,1)S(1)}, bf16[1,4,64,512]{3,2,1,0:T(8,128)(2,1)}, u32[]{:S(2)}) %copy-start.3) | copy-done | bytes 262168
  5.5 0.0 copy-start.4
  5.5 0.9 %copy-done.4 = bf16[1,128,512]{2,1,0:T(8,128)(2,1)S(1)} copy-done((bf16[1,128,512]{2,1,0:T(8,128)(2,1)S(1)}, bf16[1,128,512]{2,1,0:T(8,128)(2,1)}, u32[]{:S(2)}) %copy-start.4) | copy-done | bytes 131096
  6.4 0.0 copy-start.5
  6.4 0.8 %copy-done.5 = bf16[1,64,512]{2,1,0:T(8,128)(2,1)S(1)} copy-done((bf16[1,64,512]{2,1,0:T(8,128)(2,1)S(1)}, bf16[1,64,512]{2,1,0:T(8,128)(2,1)}, u32[]{:S(2)}) %copy-start.5) | copy-done | bytes 65560
  7.3 69.3 %diloco_step.1 = (bf16[128,512]{1,0:T(8,128)(2,1)S(1)}, bf16[128,4096]{1,0:T(8,128)(2,1)S(1)}, bf16[64,512]{1,0:T(8,128)(2,1)S(1)}, f32[4,64,512]{2,1,0:T(8,128)S(1)}, f32[4,64,512]{2,1,0:T(8,128)S(1)}) custom-call(s32[1]{0:T(128)S(6)} %copy.17.plan_ref, bf16[128,4096]{1,0:T(8,128)(2,1)S(1)} %bitcast.10, bf16[128,512]{1,0:T(8,128)(2,1)S(1)} %bitcast.12, ...), custom_call_target="tpu_custom_call" | custom-call | flops 1700000000 | bytes 7340032 | tf_op jit(solution)/shard_map/diloco_step/pallas_call | solution.py:335
  76.6 0.7 copy.18
  77.2 1.0 %copy.19 = bf16[1,128,4096]{2,1,0:T(8,128)(2,1)} copy(bf16[1,128,4096]{2,1,0:T(8,128)(2,1)S(1)} %bitcast.7) | data formatting | bytes 2097152
  78.2 0.6 copy.20
  78.8 0.8 copy.21
  79.6 0.8 copy.22
Async XLA Ops:
  1.3 1.2 %copy-start = (bf16[1,128,4096]{2,1,0:T(8,128)(2,1)S(1)}, bf16[1,128,4096]{2,1,0:T(8,128)(2,1)}, u32[]{:S(2)}) copy-start(bf16[1,128,4096]{2,1,0:T(8,128)(2,1)} %param.7) | copy-start | bytes 3145732
  2.5 1.0 %copy-start.1 = (f32[4,64,512]{2,1,0:T(8,128)S(1)}, f32[4,64,512]{2,1,0:T(8,128)}, u32[]{:S(2)}) copy-start(f32[4,64,512]{2,1,0:T(8,128)} %glob_ref.1) | copy-start | bytes 1572868
  3.5 1.0 %copy-start.2 = (f32[4,64,512]{2,1,0:T(8,128)S(1)}, f32[4,64,512]{2,1,0:T(8,128)}, u32[]{:S(2)}) copy-start(f32[4,64,512]{2,1,0:T(8,128)} %mom_ref.1) | copy-start | bytes 1572868
  4.6 0.9 %copy-start.3 = (bf16[1,4,64,512]{3,2,1,0:T(8,128)(2,1)S(1)}, bf16[1,4,64,512]{3,2,1,0:T(8,128)(2,1)}, u32[]{:S(2)}) copy-start(bf16[1,4,64,512]{3,2,1,0:T(8,128)(2,1)} %param.10) | copy-start | bytes 786436
  5.5 0.9 %copy-start.4 = (bf16[1,128,512]{2,1,0:T(8,128)(2,1)S(1)}, bf16[1,128,512]{2,1,0:T(8,128)(2,1)}, u32[]{:S(2)}) copy-start(bf16[1,128,512]{2,1,0:T(8,128)(2,1)} %param.8) | copy-start | bytes 393220
  6.4 0.8 %copy-start.5 = (bf16[1,64,512]{2,1,0:T(8,128)(2,1)S(1)}, bf16[1,64,512]{2,1,0:T(8,128)(2,1)}, u32[]{:S(2)}) copy-start(bf16[1,64,512]{2,1,0:T(8,128)(2,1)} %param.9) | copy-start | bytes 196612

commit v2 on v1

v2 whole, which is shorter than its diff:
```python
import functools

import jax
import jax.numpy as jnp
from jax import lax
from jax.experimental import pallas as pl
from jax.experimental.pallas import tpu as pltpu
from jax.sharding import PartitionSpec as P

MESH = pl.DeviceIdType.MESH
F32 = jnp.float32
BF16 = jnp.bfloat16
T = 128
F = 512
B = 64
RATE = 0.0002


def kernel(
    plan_ref, act_ref, cot_ref, w_ref, stale_ref, glob_ref, mom_ref,
    values_ref, igrad_ref, neww_ref, newg_ref, newm_ref,
    actg, cotg, wg, dwp, brs, zsum, zrs, zfar, vp, vrs, ig, vout, wout,
    stl, sel, selp, chip, rsr, sg, gin, minn, gout, mout,
    s_cot, r_cot, s_act, r_act, s_wz, r_wz, s_wb, r_wb, s_b, r_b, s_z, r_z, s_zf, r_zf,
    s_ig, r_ig, s_v, r_v, s_st, r_st, l_in, l_act, l_out,
):
    rep = lax.axis_index("replica")
    fs = lax.axis_index("fsdp")
    zl, core = rep // 2, rep % 2
    x, y, z = fs // 16, (fs // 4) % 4, fs % 4
    step_a, step_b = 16 - 12 * core, 4 + 12 * core
    a, b = x + core * (y - x), y + core * (x - y)
    wide_a, wide_b = 1024 - 768 * core, 256 + 768 * core
    zz = z % 2
    pair = z // 2

    def at_a(d):
        return (rep, ((a + d) % 4) * step_a + b * step_b + z)

    def at_b(d):
        return (rep, a * step_a + ((b + d) % 4) * step_b + z)

    z_of = (z + 1 - 2 * zz, 3 - z)

    def at_z(k):
        return (rep, x * 16 + y * 4 + z_of[k])

    def at_zl(d):
        return (((zl + d) % 4) * 2 + core, fs)

    ORDER = (1, 3, 2)
    CHUNKS = (2, 1, 3, 0)
    other_core = (zl * 2 + 1 - core, fs)

    def rdma(src, dst, send, recv, to):
        return pltpu.make_async_remote_copy(
            src_ref=src, dst_ref=dst, send_sem=send, recv_sem=recv, device_id=to, device_id_type=MESH
        )

    def rows(i, n):
        return pl.ds(pl.multiple_of(i * n, n), n)

    def channels(aa, bb, half):
        zp = half * pair + (1 - half) * (1 - pair)
        return pl.ds(pl.multiple_of(aa * wide_a + bb * wide_b + zp * 128, 128), 128)

    def lanes(bb):
        return pl.ds(pl.multiple_of(bb * 128, 128), 128)

    loads = [
        pltpu.make_async_copy(stale_ref, stl, l_in.at[0]),
        pltpu.make_async_copy(glob_ref, gin, l_in.at[1]),
        pltpu.make_async_copy(mom_ref, minn, l_in.at[2]),
        pltpu.make_async_copy(cot_ref, cotg.at[rows(a, T)], l_in.at[3]),
        pltpu.make_async_copy(w_ref, wg.at[1, pl.ds(pl.multiple_of(b * 128 + zz * 64, 64), B)], l_in.at[4]),
    ]
    for c in loads:
        c.start()
    def act_own(half, j):
        bb = (b + CHUNKS[j]) % 4
        return pltpu.make_async_copy(
            act_ref.at[:, channels(a, bb, half)], actg.at[half, rows(a, T), lanes(bb)], l_act.at[half, j]
        )

    for half in (0, 1):
        for j in range(4):
            act_own(half, j).start()

    barrier = pltpu.get_barrier_semaphore()
    greet = [at_a(d) for d in (1, 2, 3)] + [at_b(d) for d in (1, 2, 3)] + [at_z(k) for k in range(2)]
    greet += [at_zl(d) for d in (1, 2, 3)] + [other_core]
    for to in greet:
        pl.semaphore_signal(barrier, inc=1, device_id=to, device_id_type=MESH)
    pl.semaphore_wait(barrier, len(greet))

    cots = [rdma(cot_ref, cotg.at[rows(a, T)], s_cot.at[d - 1], r_cot.at[d - 1], at_a(d)) for d in (1, 2, 3)]
    for d in ORDER:
        cots[d - 1].start()

    def w_rows(zpar):
        return pl.ds(pl.multiple_of(b * 128 + zpar * 64, 64), B)

    wz = [
        rdma(w_ref, wg.at[1 if k == 0 else 0, w_rows(zz)], s_wz.at[k], r_wz.at[k], at_z(k)) for k in range(2)
    ]
    for k in range(2):
        wz[k].start()
    slots = ((1, zz), (1, 1 - zz), (0, 1 - zz), (0, zz))

    def wb(slot, d):
        half, zpar = slots[slot]
        there = wg.at[half, w_rows(zpar)]
        return rdma(w_ref if slot == 0 else there, there, s_wb.at[slot, d - 1], r_wb.at[slot, d - 1], at_b(d))

    for d in ORDER:
        wb(0, d).start()

    def act_send(half, j, d):
        bb = (b + CHUNKS[j]) % 4
        return rdma(
            act_ref.at[:, channels((a + d) % 4, bb, half)],
            actg.at[half, rows(a, T), lanes(bb)],
            s_act.at[half, j, d - 1],
            r_act.at[half, j, d - 1],
            at_a(d),
        )

    for half in (0, 1):
        for j in range(4):
            for d in ORDER:
                act_send(half, j, d).start()

    frag = plan_ref[0] % 4
    loads[0].wait()
    picked = jnp.zeros((B, F), F32)
    for k in range(4):
        picked = jnp.where(frag == k, stl[k].astype(F32), picked)
    sel[...] = picked.astype(BF16)
    to_core = rdma(sel, selp, s_st.at[0], r_st.at[0], other_core)
    to_core.start()
    to_core.wait_recv()
    chip[...] = (sel[...].astype(F32) + selp[...].astype(F32)).reshape(4, 2, 8, F)
    scatter = [
        rdma(chip.at[(zl + d) % 4, core], rsr.at[d - 1], s_st.at[d], r_st.at[d], at_zl(d)) for d in (1, 2, 3)
    ]
    for c in scatter:
        c.start()

    def b_send(half, zpar, j):
        to = (b + CHUNKS[j]) % 4
        return rdma(
            dwp.at[half, pl.ds(pl.multiple_of(to * 128 + zpar * 64, 64), B)],
            brs.at[half, zpar, j],
            s_b.at[half, zpar, j],
            r_b.at[half, zpar, j],
            at_b(CHUNKS[j]),
        )

    def weight_grad(half, first):
        for j in range(4):
            act_own(half, j).wait()
            for d in ORDER:
                act_send(half, j, d).wait_recv()
            cols = lanes((b + CHUNKS[j]) % 4)
            dwp[half, cols] = lax.dot_general(
                actg[half, :, cols], cotg[...], (((0,), (0,)), ((), ())), preferred_element_type=F32
            )
            if j < 3:
                b_send(half, first, j).start()
                b_send(half, 1 - first, j).start()

    loads[3].wait()
    for c in cots:
        c.wait_recv()
    weight_grad(0, zz)

    def part(i, zpar, h):
        return wg.at[i, pl.ds(pl.multiple_of(b * 128 + zpar * 64 + h * 32, 32), B // 2)]

    wz2 = [
        rdma(part(1 - h, 1 - zz, h), part(0, 1 - zz, h), s_wz.at[2 + h], r_wz.at[2 + h], at_z(1 - h)) for h in (0, 1)
    ]

    def pass_on(slot):
        for d in ORDER:
            wb(slot, d).start()

    for k in (0, 1):
        wz[k].wait_recv()
        wz2[k].start()
        pass_on(k + 1)

    for c in scatter:
        c.wait_recv()
    sg[zl, core] = chip[zl, core] + rsr[0] + rsr[1] + rsr[2]
    spread = [
        rdma(sg.at[zl, core], sg.at[zl, core], s_st.at[3 + d], r_st.at[3 + d], at_zl(d)) for d in (1, 2, 3)
    ]
    for c in spread:
        c.start()

    weight_grad(1, 1 - zz)
    for c in wz2:
        c.wait_recv()
    pass_on(3)

    def halves(h):
        return pl.ds(h * 32, B // 2)

    def z_far(h):
        return rdma(zsum.at[2, halves(h)], zfar.at[h], s_zf.at[h], r_zf.at[h], at_z(1 - h))

    def z_send(k, h):
        return rdma(zsum.at[k, halves(h)], zrs.at[k, halves(h)], s_z.at[k, h], r_z.at[k, h], at_z(k))

    def over_b(half, zpar):
        for j in range(3):
            b_send(half, zpar, j).wait_recv()
        mine = dwp[half, pl.ds(pl.multiple_of(b * 128 + zpar * 64, 64), B)]
        return mine + brs[half, zpar, 0] + brs[half, zpar, 1] + brs[half, zpar, 2]

    def z_add(h):
        z_far(h).wait_recv()
        zsum[h, halves(h)] = zsum[h, halves(h)] + zfar[h]
        z_send(h, h).start()

    zsum[2] = over_b(0, zz)
    z_far(0).start()
    z_far(1).start()

    def ig_send(half, yy, d):
        return rdma(
            ig.at[half, rows((a + d) % 4, T), pl.ds(yy * 128, 128)],
            igrad_ref.at[:, channels(a, yy, half)],
            s_ig.at[half, d - 1],
            r_ig.at[half, d - 1],
            at_a(d),
        )

    def input_grad(half):
        ig[half] = lax.dot_general(
            cotg[...], wg[half], (((1,), (1,)), ((), ())), preferred_element_type=F32
        ).astype(BF16)
        for yy in range(4):
            for d in ORDER:
                ig_send(half, yy, d).start()
            pltpu.make_async_copy(
                ig.at[half, rows(a, T), pl.ds(yy * 128, 128)], igrad_ref.at[:, channels(a, yy, half)], l_out.at[half]
            ).start()

    loads[4].wait()
    for slot in (0, 1):
        for d in ORDER:
            wb(slot, d).wait_recv()
    input_grad(1)

    zsum[1] = over_b(0, 1 - zz)
    z_send(1, 0).start()
    zsum[0] = over_b(1, 1 - zz)
    z_send(0, 1).start()

    for slot in (2, 3):
        for d in ORDER:
            wb(slot, d).wait_recv()
    input_grad(0)

    vp[...] = jnp.dot(actg[0], wg[0], preferred_element_type=F32) + jnp.dot(
        actg[1], wg[1], preferred_element_type=F32
    )

    def v_send(d):
        return rdma(vp.at[rows((a + d) % 4, T)], vrs.at[d - 1], s_v.at[d - 1], r_v.at[d - 1], at_a(d))

    for d in ORDER:
        v_send(d).start()

    z_add(1)
    z_add(0)

    for c in spread:
        c.wait_recv()
    across = rdma(sg.at[:, core], sg.at[:, core], s_st.at[7], r_st.at[7], other_core)
    across.start()
    across.wait_recv()
    loads[1].wait()
    loads[2].wait()
    old = jnp.zeros((B, F), F32)
    moment = jnp.zeros((B, F), F32)
    for k in range(4):
        old = jnp.where(frag == k, gin[k], old)
        moment = jnp.where(frag == k, minn[k], moment)
    mean = old - sg[...].reshape(B, F) / 8.0
    moment = 0.9 * moment + mean
    new = old - 0.7 * (mean + 0.9 * moment)
    for k in range(4):
        gout[k] = jnp.where(frag == k, new, gin[k])
        mout[k] = jnp.where(frag == k, moment, minn[k])
    stores = [
        pltpu.make_async_copy(gout, newg_ref, l_out.at[2]),
        pltpu.make_async_copy(mout, newm_ref, l_out.at[3]),
    ]
    stores[0].start()
    stores[1].start()

    zsum[3] = over_b(1, zz)

    for d in ORDER:
        v_send(d).wait_recv()
    vout[...] = (vp[rows(a, T)] + vrs[0] + vrs[1] + vrs[2]).astype(BF16)
    stores.append(pltpu.make_async_copy(vout, values_ref, l_out.at[4]))
    stores[2].start()

    for k in (0, 1):
        for h in (0, 1):
            z_send(k, h).wait_recv()
    grad = zsum[3] + zrs[0] + zrs[1]
    inner = wg[1, w_rows(zz)].astype(F32) - RATE * grad
    picked = jnp.zeros((B, F), F32)
    for k in range(4):
        picked = jnp.where(frag == k, gout[k], picked)
    wout[...] = (0.5 * inner + 0.5 * picked).astype(BF16)
    stores.append(pltpu.make_async_copy(wout, neww_ref, l_out.at[5]))
    stores[3].start()

    for half in (0, 1):
        landed = igrad_ref.at[:, pl.ds(0, 512)]
        for d in (1, 2, 3):
            own = ig.at[half, rows((a + d) % 4, T)]
            back = rdma(own, landed, s_ig.at[half, d - 1], r_ig.at[half, d - 1], at_a(d))
            back.wait_recv()
            back.wait_send()
            for j in range(4):
                act_send(half, j, d).wait_send()
        pltpu.make_async_copy(ig.at[half, rows(a, T)], landed, l_out.at[half]).wait()
    for c in cots + wz + wz2 + scatter + spread + [to_core, across]:
        c.wait_send()
    for d in (1, 2, 3):
        v_send(d).wait_send()
        for slot in range(4):
            wb(slot, d).wait_send()
        for half in (0, 1):
            for zpar in (0, 1):
                b_send(half, zpar, d - 1).wait_send()
    for k in (0, 1):
        z_far(k).wait_send()
        for h in (0, 1):
            z_send(k, h).wait_send()
    for c in stores:
        c.wait()


def hand_out(*refs):
    ins, outs, vmem, arrived, left = refs[:5], refs[5:10], refs[10:15], refs[15], refs[16]
    come = [pltpu.make_async_copy(ins[i], vmem[i], arrived.at[i]) for i in range(5)]
    go = [pltpu.make_async_copy(vmem[i], outs[i], left.at[i]) for i in range(5)]
    for i in (1, 3, 4, 0, 2):
        come[i].start()
    for i in (1, 3, 4, 0, 2):
        come[i].wait()
        go[i].start()
    for i in range(5):
        go[i].wait()


def per_device(activations, cotangent, weights, stale_params, global_params, momentum, plan):
    anywhere = pl.BlockSpec(memory_space=pl.ANY)
    dma = pltpu.SemaphoreType.DMA
    outs = pl.pallas_call(
        kernel,
        name="diloco_step",
        out_shape=(
            jax.ShapeDtypeStruct((T, F), BF16),
            jax.ShapeDtypeStruct((T, 4096), BF16),
            jax.ShapeDtypeStruct((B, F), BF16),
            jax.ShapeDtypeStruct((4, B, F), F32),
            jax.ShapeDtypeStruct((4, B, F), F32),
        ),
        in_specs=[pl.BlockSpec(memory_space=pltpu.SMEM)] + [anywhere] * 6,
        out_specs=(anywhere,) * 5,
        scratch_shapes=[
            pltpu.VMEM((2, 512, 512), BF16),
            pltpu.VMEM((512, F), BF16),
            pltpu.VMEM((2, 512, F), BF16),
            pltpu.VMEM((2, 512, F), F32),
            pltpu.VMEM((2, 2, 3, B, F), F32),
            pltpu.VMEM((4, B, F), F32),
            pltpu.VMEM((2, B, F), F32),
            pltpu.VMEM((2, B // 2, F), F32),
            pltpu.VMEM((512, F), F32),
            pltpu.VMEM((3, T, F), F32),
            pltpu.VMEM((2, 512, 512), BF16),
            pltpu.VMEM((T, F), BF16),
            pltpu.VMEM((B, F), BF16),
            pltpu.VMEM((4, B, F), BF16),
            pltpu.VMEM((B, F), BF16),
            pltpu.VMEM((B, F), BF16),
            pltpu.VMEM((4, 2, 8, F), F32),
            pltpu.VMEM((3, 8, F), F32),
            pltpu.VMEM((4, 2, 8, F), F32),
            pltpu.VMEM((4, B, F), F32),
            pltpu.VMEM((4, B, F), F32),
            pltpu.VMEM((4, B, F), F32),
            pltpu.VMEM((4, B, F), F32),
            dma((3,)), dma((3,)),
            dma((2, 4, 3)), dma((2, 4, 3)),
            dma((4,)), dma((4,)),
            dma((4, 3)), dma((4, 3)),
            dma((2, 2, 3)), dma((2, 2, 3)),
            dma((2, 2)), dma((2, 2)),
            dma((2,)), dma((2,)),
            dma((2, 3)), dma((2, 3)),
            dma((3,)), dma((3,)),
            dma((8,)), dma((8,)),
            dma((5,)), dma((2, 4)), dma((6,)),
        ],
        compiler_params=pltpu.CompilerParams(
            collective_id=0, has_side_effects=True, vmem_limit_bytes=60 << 20
        ),
        cost_estimate=pl.CostEstimate(flops=1_700_000_000, bytes_accessed=7 << 20, transcendentals=0),
    )(plan, activations[0], cotangent[0], weights[0], stale_params[0], global_params, momentum)
    values, igrad, neww, newg, newm = pl.pallas_call(
        hand_out,
        name="hand_out",
        out_shape=tuple(jax.ShapeDtypeStruct(o.shape, o.dtype) for o in outs),
        in_specs=[anywhere] * 5,
        out_specs=(anywhere,) * 5,
        scratch_shapes=[pltpu.VMEM(o.shape, o.dtype) for o in outs] + [dma((5,)), dma((5,))],
        compiler_params=pltpu.CompilerParams(vmem_limit_bytes=60 << 20),
    )(*outs)
    return (values[None], igrad[None], neww[None], newg, newm)


def solution(mesh):
    placed = (
        P("replica", "fsdp", None),
        P("replica", "fsdp", None),
        P("replica", "fsdp", None),
        P("replica", None, "fsdp", None),
        P(None, "fsdp", None),
        P(None, "fsdp", None),
        P(),
    )
    return jax.shard_map(
        per_device,
        mesh=mesh,
        in_specs=placed,
        out_specs=(
            P("replica", "fsdp", None),
            P("replica", "fsdp", None),
            P("replica", "fsdp", None),
            P(None, "fsdp", None),
            P(None, "fsdp", None),
        ),
        check_vma=False,
    )
```

time: 80.8 us -> 64.2 us (0.79)
  the two profiles are of different devices: /device:TPU:32 before, /device:TPU:1 now
where the time goes in v2:
time: 64.2 us; the launch traced here: 64 us
  Pallas kernels  62.7 us (98%)
  between operations  1.29 us (2%)
    pallas_call x1, Pallas kernels, per_device(): pl.pallas_call(kernel, name='diloco_step', out_shape=(jax.ShapeDtypeStruc...  60 us
    pallas_call x1, Pallas kernels, per_device(): pl.pallas_call(hand_out, name='hand_out', out_shape=tuple((jax.ShapeDtype...  2.68 us

profile of v2, /device:TPU:1, one launch (start us, length us, event | category | flops | bytes accessed | tf_op | source)
XLA Modules:
  0.0 64.0 jit_solution(13861806164511071870)
XLA Ops:
  1.3 60.0 %diloco_step.1 = (bf16[128,512]{1,0:T(8,128)(2,1)}, bf16[128,4096]{1,0:T(8,128)(2,1)}, bf16[64,512]{1,0:T(8,128)(2,1)}, f32[4,64,512]{2,1,0:T(8,128)}, f32[4,64,512]{2,1,0:T(8,128)}) custom-call(s32[1]{0:T(128)S(6)} %copy.12.plan_ref, bf16[128,4096]{1,0:T(8,128)(2,1)} %bitcast.7, bf16[128,512]{1,0:T(8,128)(2,1)} %bitcast.10, bf16[64,512]{1,0:T(8,128)(2,1)} %bitcast.12, ...), custom_call_target="tpu_custom_call" | custom-call | flops 1700000000 | bytes 7340032 | tf_op jit(solution)/shard_map/diloco_step/pallas_call | solution.py:368
  61.3 2.7 %hand_out.1 = (bf16[128,512]{1,0:T(8,128)(2,1)}, bf16[128,4096]{1,0:T(8,128)(2,1)}, bf16[64,512]{1,0:T(8,128)(2,1)}, f32[4,64,512]{2,1,0:T(8,128)}, f32[4,64,512]{2,1,0:T(8,128)}) custom-call(bf16[128,512]{1,0:T(8,128)(2,1)} %get-tuple-element.15.refs_0_, bf16[128,4096]{1,0:T(8,128)(2,1)} %get-tuple-element.16.refs_1_, ...), custom_call_target="tpu_custom_call" | custom-call | tf_op jit(solution)/shard_map/hand_out/pallas_call | solution.py:421

commit v3 on v2

--- a/solution.py
+++ b/solution.py
@@ -19,9 +19,9 @@
 def kernel(
     plan_ref, act_ref, cot_ref, w_ref, stale_ref, glob_ref, mom_ref,
     values_ref, igrad_ref, neww_ref, newg_ref, newm_ref,
-    actg, cotg, wg, dwp, brs, zsum, zrs, zfar, vp, vrs, ig, vout, wout,
+    actg, cotg, wg, dwp, brs, bfar, zsum, zrs, zfar, vp, vrs, ig, vout, wout,
     stl, sel, selp, chip, rsr, sg, gin, minn, gout, mout,
-    s_cot, r_cot, s_act, r_act, s_wz, r_wz, s_wb, r_wb, s_b, r_b, s_z, r_z, s_zf, r_zf,
+    s_cot, r_cot, s_act, r_act, s_wz, r_wz, s_wb, r_wb, s_wbf, r_wbf, s_b, r_b, s_bf, r_bf, s_z, r_z, s_zf, r_zf,
     s_ig, r_ig, s_v, r_v, s_st, r_st, l_in, l_act, l_out,
 ):
     rep = lax.axis_index("replica")
@@ -49,6 +49,7 @@
         return (((zl + d) % 4) * 2 + core, fs)
 
     ORDER = (1, 3, 2)
+    NEAR = (1, 3)
     CHUNKS = (2, 1, 3, 0)
     other_core = (zl * 2 + 1 - core, fs)
 
@@ -107,13 +108,28 @@
         wz[k].start()
     slots = ((1, zz), (1, 1 - zz), (0, 1 - zz), (0, zz))
 
-    def wb(slot, d):
+    def wb(slot, k):
         half, zpar = slots[slot]
         there = wg.at[half, w_rows(zpar)]
-        return rdma(w_ref if slot == 0 else there, there, s_wb.at[slot, d - 1], r_wb.at[slot, d - 1], at_b(d))
-
-    for d in ORDER:
-        wb(0, d).start()
+        return rdma(w_ref if slot == 0 else there, there, s_wb.at[slot, k], r_wb.at[slot, k], at_b(NEAR[k]))
+
+    def wb_far(slot, h):
+        half, zpar = slots[slot]
+        owner = (b + 3 + 2 * h) % 4
+        there = wg.at[half, pl.ds(pl.multiple_of(owner * 128 + zpar * 64 + h * 32, 32), B // 2)]
+        return rdma(there, there, s_wbf.at[slot, h], r_wbf.at[slot, h], at_b(NEAR[h]))
+
+    def wb_on(slot):
+        for h in (0, 1):
+            wb(slot, h).wait_recv()
+            wb_far(slot, h).start()
+
+    def wb_all(slot):
+        for h in (0, 1):
+            wb_far(slot, h).wait_recv()
+
+    for k in (0, 1):
+        wb(0, k).start()
 
     def act_send(half, j, d):
         bb = (b + CHUNKS[j]) % 4
@@ -146,15 +162,33 @@
     for c in scatter:
         c.start()
 
-    def b_send(half, zpar, j):
-        to = (b + CHUNKS[j]) % 4
+    def halves(h):
+        return pl.ds(h * 32, B // 2)
+
+    def chunk(half, off, zpar, h):
+        to = (b + off) % 4
+        return dwp.at[half, pl.ds(pl.multiple_of(to * 128 + zpar * 64 + h * 32, 32), B // 2)]
+
+    def b_far(half, zpar, h):
         return rdma(
-            dwp.at[half, pl.ds(pl.multiple_of(to * 128 + zpar * 64, 64), B)],
-            brs.at[half, zpar, j],
-            s_b.at[half, zpar, j],
-            r_b.at[half, zpar, j],
-            at_b(CHUNKS[j]),
+            chunk(half, 2, zpar, h), bfar.at[half, zpar, h], s_bf.at[half, zpar, h], r_bf.at[half, zpar, h], at_b(NEAR[h])
         )
+
+    def b_send(half, zpar, k, h):
+        return rdma(
+            chunk(half, NEAR[k], zpar, h),
+            brs.at[half, zpar, k, halves(h)],
+            s_b.at[half, zpar, k, h],
+            r_b.at[half, zpar, k, h],
+            at_b(NEAR[k]),
+        )
+
+    def b_add(half, zpar):
+        for h in (0, 1):
+            b_far(half, zpar, h).wait_recv()
+            there = chunk(half, NEAR[h], zpar, h)
+            there[...] = there[...] + bfar[half, zpar, h]
+            b_send(half, zpar, h, h).start()
 
     def weight_grad(half, first):
         for j in range(4):
@@ -165,9 +199,12 @@
             dwp[half, cols] = lax.dot_general(
                 actg[half, :, cols], cotg[...], (((0,), (0,)), ((), ())), preferred_element_type=F32
             )
-            if j < 3:
-                b_send(half, first, j).start()
-                b_send(half, 1 - first, j).start()
+            for zpar in (first, 1 - first):
+                if j == 0:
+                    for h in (0, 1):
+                        b_far(half, zpar, h).start()
+                elif j < 3:
+                    b_send(half, zpar, j - 1, 2 - j).start()
 
     loads[3].wait()
     for c in cots:
@@ -182,8 +219,8 @@
     ]
 
     def pass_on(slot):
-        for d in ORDER:
-            wb(slot, d).start()
+        for k in (0, 1):
+            wb(slot, k).start()
 
     for k in (0, 1):
         wz[k].wait_recv()
@@ -199,13 +236,17 @@
     for c in spread:
         c.start()
 
+    wb_on(0)
+    b_add(0, zz)
+    b_add(0, 1 - zz)
     weight_grad(1, 1 - zz)
     for c in wz2:
         c.wait_recv()
     pass_on(3)
-
-    def halves(h):
-        return pl.ds(h * 32, B // 2)
+    wb_on(1)
+    wb_on(2)
+    b_add(1, 1 - zz)
+    b_add(1, zz)
 
     def z_far(h):
         return rdma(zsum.at[2, halves(h)], zfar.at[h], s_zf.at[h], r_zf.at[h], at_z(1 - h))
@@ -214,10 +255,11 @@
         return rdma(zsum.at[k, halves(h)], zrs.at[k, halves(h)], s_z.at[k, h], r_z.at[k, h], at_z(k))
 
     def over_b(half, zpar):
-        for j in range(3):
-            b_send(half, zpar, j).wait_recv()
+        for k in (0, 1):
+            for h in (0, 1):
+                b_send(half, zpar, k, h).wait_recv()
         mine = dwp[half, pl.ds(pl.multiple_of(b * 128 + zpar * 64, 64), B)]
-        return mine + brs[half, zpar, 0] + brs[half, zpar, 1] + brs[half, zpar, 2]
+        return mine + brs[half, zpar, 0] + brs[half, zpar, 1]
 
     def z_add(h):
         z_far(h).wait_recv()
@@ -249,19 +291,18 @@
             ).start()
 
     loads[4].wait()
-    for slot in (0, 1):
-        for d in ORDER:
-            wb(slot, d).wait_recv()
-    input_grad(1)
-
+    wb_all(0)
+    wb_all(1)
+
+    wb_on(3)
     zsum[1] = over_b(0, 1 - zz)
     z_send(1, 0).start()
     zsum[0] = over_b(1, 1 - zz)
     z_send(0, 1).start()
-
-    for slot in (2, 3):
-        for d in ORDER:
-            wb(slot, d).wait_recv()
+    input_grad(1)
+
+    wb_all(2)
+    wb_all(3)
     input_grad(0)
 
     vp[...] = jnp.dot(actg[0], wg[0], preferred_element_type=F32) + jnp.dot(
@@ -336,11 +377,16 @@
         c.wait_send()
     for d in (1, 2, 3):
         v_send(d).wait_send()
-        for slot in range(4):
-            wb(slot, d).wait_send()
-        for half in (0, 1):
-            for zpar in (0, 1):
-                b_send(half, zpar, d - 1).wait_send()
+    for slot in range(4):
+        for k in (0, 1):
+            wb(slot, k).wait_send()
+            wb_far(slot, k).wait_send()
+    for half in (0, 1):
+        for zpar in (0, 1):
+            for h in (0, 1):
+                b_far(half, zpar, h).wait_send()
+                for k in (0, 1):
+                    b_send(half, zpar, k, h).wait_send()
     for k in (0, 1):
         z_far(k).wait_send()
         for h in (0, 1):
@@ -382,7 +428,8 @@
             pltpu.VMEM((512, F), BF16),
             pltpu.VMEM((2, 512, F), BF16),
             pltpu.VMEM((2, 512, F), F32),
-            pltpu.VMEM((2, 2, 3, B, F), F32),
+            pltpu.VMEM((2, 2, 2, B, F), F32),
+            pltpu.VMEM((2, 2, 2, B // 2, F), F32),
             pltpu.VMEM((4, B, F), F32),
             pltpu.VMEM((2, B, F), F32),
             pltpu.VMEM((2, B // 2, F), F32),
@@ -404,8 +451,10 @@
             dma((3,)), dma((3,)),
             dma((2, 4, 3)), dma((2, 4, 3)),
             dma((4,)), dma((4,)),
-            dma((4, 3)), dma((4, 3)),
-            dma((2, 2, 3)), dma((2, 2, 3)),
+            dma((4, 2)), dma((4, 2)),
+            dma((4, 2)), dma((4, 2)),
+            dma((2, 2, 2, 2)), dma((2, 2, 2, 2)),
+            dma((2, 2, 2)), dma((2, 2, 2)),
             dma((2, 2)), dma((2, 2)),
             dma((2,)), dma((2,)),
             dma((2, 3)), dma((2, 3)),

time: 64.2 us -> 60.4 us (0.941)
  Pallas kernels: 62.7 us -> 59 us
    pallas_call x1, Pallas kernels: 60 us -> 56.3 us  [per_device(): pl.pallas_call(kernel, name='diloco_step', out_shape=(jax.ShapeDtypeStruc...]
where the time goes in v3:
time: 60.4 us; the launch traced here: 60.2 us
  Pallas kernels  59 us (98%)
  between operations  1.29 us (2%)
    pallas_call x1, Pallas kernels, per_device(): pl.pallas_call(kernel, name='diloco_step', out_shape=(jax.ShapeDtypeStruc...  56.3 us
    pallas_call x1, Pallas kernels, per_device(): pl.pallas_call(hand_out, name='hand_out', out_shape=tuple((jax.ShapeDtype...  2.68 us

profile of v3, /device:TPU:1, one launch (start us, length us, event | category | flops | bytes accessed | tf_op | source)
XLA Modules:
  0.0 60.2 jit_solution(2688493149423758712)
XLA Ops:
  1.3 56.3 %diloco_step.1 = (bf16[128,512]{1,0:T(8,128)(2,1)}, bf16[128,4096]{1,0:T(8,128)(2,1)}, bf16[64,512]{1,0:T(8,128)(2,1)}, f32[4,64,512]{2,1,0:T(8,128)}, f32[4,64,512]{2,1,0:T(8,128)}) custom-call(s32[1]{0:T(128)S(6)} %copy.12.plan_ref, bf16[128,4096]{1,0:T(8,128)(2,1)} %bitcast.7, bf16[128,512]{1,0:T(8,128)(2,1)} %bitcast.10, bf16[64,512]{1,0:T(8,128)(2,1)} %bitcast.12, ...), custom_call_target="tpu_custom_call" | custom-call | flops 1700000000 | bytes 7340032 | tf_op jit(solution)/shard_map/diloco_step/pallas_call | solution.py:414
  57.6 2.7 %hand_out.1 = (bf16[128,512]{1,0:T(8,128)(2,1)}, bf16[128,4096]{1,0:T(8,128)(2,1)}, bf16[64,512]{1,0:T(8,128)(2,1)}, f32[4,64,512]{2,1,0:T(8,128)}, f32[4,64,512]{2,1,0:T(8,128)}) custom-call(bf16[128,512]{1,0:T(8,128)(2,1)} %get-tuple-element.15.refs_0_, bf16[128,4096]{1,0:T(8,128)(2,1)} %get-tuple-element.16.refs_1_, ...), custom_call_target="tpu_custom_call" | custom-call | tf_op jit(solution)/shard_map/hand_out/pallas_call | solution.py:470

commit v4 on v3

--- a/solution.py
+++ b/solution.py
@@ -19,9 +19,9 @@
 def kernel(
     plan_ref, act_ref, cot_ref, w_ref, stale_ref, glob_ref, mom_ref,
     values_ref, igrad_ref, neww_ref, newg_ref, newm_ref,
-    actg, cotg, wg, dwp, brs, bfar, zsum, zrs, zfar, vp, vrs, ig, vout, wout,
+    actg, cotg, wg, dwp, brs, bfar, bdir, zsum, zrs, zfar, vp, vrs, ig, vout, wout,
     stl, sel, selp, chip, rsr, sg, gin, minn, gout, mout,
-    s_cot, r_cot, s_act, r_act, s_wz, r_wz, s_wb, r_wb, s_wbf, r_wbf, s_b, r_b, s_bf, r_bf, s_z, r_z, s_zf, r_zf,
+    s_cot, r_cot, s_act, r_act, s_wz, r_wz, s_wb, r_wb, s_wbf, r_wbf, s_b, r_b, s_bf, r_bf, s_bd, r_bd, s_z, r_z, s_zf, r_zf,
     s_ig, r_ig, s_v, r_v, s_st, r_st, l_in, l_act, l_out,
 ):
     rep = lax.axis_index("replica")
@@ -190,6 +190,16 @@
             there[...] = there[...] + bfar[half, zpar, h]
             b_send(half, zpar, h, h).start()
 
+    def b_direct(h, j):
+        return rdma(
+            chunk(1, CHUNKS[j], 1 - zz, h), bdir.at[h, j], s_bd.at[h, j], r_bd.at[h, j], at_b(CHUNKS[j])
+        )
+
+    def over_b_direct(h):
+        for j in range(3):
+            b_direct(h, j).wait_recv()
+        return chunk(1, 0, 1 - zz, h)[...] + bdir[h, 0] + bdir[h, 1] + bdir[h, 2]
+
     def weight_grad(half, first):
         for j in range(4):
             act_own(half, j).wait()
@@ -199,12 +209,15 @@
             dwp[half, cols] = lax.dot_general(
                 actg[half, :, cols], cotg[...], (((0,), (0,)), ((), ())), preferred_element_type=F32
             )
-            for zpar in (first, 1 - first):
+            for zpar in (first, 1 - first)[half:]:
                 if j == 0:
                     for h in (0, 1):
                         b_far(half, zpar, h).start()
                 elif j < 3:
                     b_send(half, zpar, j - 1, 2 - j).start()
+            if half == 1 and j < 3:
+                for h in (1, 0):
+                    b_direct(h, j).start()
 
     loads[3].wait()
     for c in cots:
@@ -245,8 +258,6 @@
     pass_on(3)
     wb_on(1)
     wb_on(2)
-    b_add(1, 1 - zz)
-    b_add(1, zz)
 
     def z_far(h):
         return rdma(zsum.at[2, halves(h)], zfar.at[h], s_zf.at[h], r_zf.at[h], at_z(1 - h))
@@ -297,8 +308,10 @@
     wb_on(3)
     zsum[1] = over_b(0, 1 - zz)
     z_send(1, 0).start()
-    zsum[0] = over_b(1, 1 - zz)
+    zsum[0, halves(1)] = over_b_direct(1)
     z_send(0, 1).start()
+    zsum[0, halves(0)] = over_b_direct(0)
+    b_add(1, zz)
     input_grad(1)
 
     wb_all(2)
@@ -381,12 +394,14 @@
         for k in (0, 1):
             wb(slot, k).wait_send()
             wb_far(slot, k).wait_send()
-    for half in (0, 1):
-        for zpar in (0, 1):
-            for h in (0, 1):
-                b_far(half, zpar, h).wait_send()
-                for k in (0, 1):
-                    b_send(half, zpar, k, h).wait_send()
+    for half, zpar in ((0, zz), (0, 1 - zz), (1, zz)):
+        for h in (0, 1):
+            b_far(half, zpar, h).wait_send()
+            for k in (0, 1):
+                b_send(half, zpar, k, h).wait_send()
+    for h in (0, 1):
+        for j in range(3):
+            b_direct(h, j).wait_send()
     for k in (0, 1):
         z_far(k).wait_send()
         for h in (0, 1):
@@ -397,15 +412,16 @@
 
 def hand_out(*refs):
     ins, outs, vmem, arrived, left = refs[:5], refs[5:10], refs[10:15], refs[15], refs[16]
-    come = [pltpu.make_async_copy(ins[i], vmem[i], arrived.at[i]) for i in range(5)]
-    go = [pltpu.make_async_copy(vmem[i], outs[i], left.at[i]) for i in range(5)]
-    for i in (1, 3, 4, 0, 2):
-        come[i].start()
-    for i in (1, 3, 4, 0, 2):
-        come[i].wait()
-        go[i].start()
-    for i in range(5):
-        go[i].wait()
+    parts = [(1, pl.ds(k * 32, 32)) for k in range(4)] + [(3, slice(None)), (4, slice(None)), (0, slice(None)), (2, slice(None))]
+    come = [pltpu.make_async_copy(ins[i].at[p], vmem[i].at[p], arrived.at[n]) for n, (i, p) in enumerate(parts)]
+    go = [pltpu.make_async_copy(vmem[i].at[p], outs[i].at[p], left.at[n]) for n, (i, p) in enumerate(parts)]
+    for c in come:
+        c.start()
+    for c, d in zip(come, go):
+        c.wait()
+        d.start()
+    for d in go:
+        d.wait()
 
 
 def per_device(activations, cotangent, weights, stale_params, global_params, momentum, plan):
@@ -430,6 +446,7 @@
             pltpu.VMEM((2, 512, F), F32),
             pltpu.VMEM((2, 2, 2, B, F), F32),
             pltpu.VMEM((2, 2, 2, B // 2, F), F32),
+            pltpu.VMEM((2, 3, B // 2, F), F32),
             pltpu.VMEM((4, B, F), F32),
             pltpu.VMEM((2, B, F), F32),
             pltpu.VMEM((2, B // 2, F), F32),
@@ -455,6 +472,7 @@
             dma((4, 2)), dma((4, 2)),
             dma((2, 2, 2, 2)), dma((2, 2, 2, 2)),
             dma((2, 2, 2)), dma((2, 2, 2)),
+            dma((2, 3)), dma((2, 3)),
             dma((2, 2)), dma((2, 2)),
             dma((2,)), dma((2,)),
             dma((2, 3)), dma((2, 3)),
@@ -473,7 +491,7 @@
         out_shape=tuple(jax.ShapeDtypeStruct(o.shape, o.dtype) for o in outs),
         in_specs=[anywhere] * 5,
         out_specs=(anywhere,) * 5,
-        scratch_shapes=[pltpu.VMEM(o.shape, o.dtype) for o in outs] + [dma((5,)), dma((5,))],
+        scratch_shapes=[pltpu.VMEM(o.shape, o.dtype) for o in outs] + [dma((8,)), dma((8,))],
         compiler_params=pltpu.CompilerParams(vmem_limit_bytes=60 << 20),
     )(*outs)
     return (values[None], igrad[None], neww[None], newg, newm)

time: 60.4 us -> 59.6 us (0.987)
  Pallas kernels: 59 us -> 58.2 us
    pallas_call x1, Pallas kernels: 56.3 us -> 55.7 us  [per_device(): pl.pallas_call(kernel, name='diloco_step', out_shape=(jax.ShapeDtypeStruc...]
where the time goes in v4:
time: 59.6 us; the launch traced here: 59.5 us
  Pallas kernels  58.2 us (98%)
  between operations  1.29 us (2%)
    pallas_call x1, Pallas kernels, per_device(): pl.pallas_call(kernel, name='diloco_step', out_shape=(jax.ShapeDtypeStruc...  55.7 us
    pallas_call x1, Pallas kernels, per_device(): pl.pallas_call(hand_out, name='hand_out', out_shape=tuple((jax.ShapeDtype...  2.52 us

profile of v4, /device:TPU:1, one launch (start us, length us, event | category | flops | bytes accessed | tf_op | source)
XLA Modules:
  0.0 59.5 jit_solution(11981540768764092979)
XLA Ops:
  1.3 55.7 %diloco_step.1 = (bf16[128,512]{1,0:T(8,128)(2,1)}, bf16[128,4096]{1,0:T(8,128)(2,1)}, bf16[64,512]{1,0:T(8,128)(2,1)}, f32[4,64,512]{2,1,0:T(8,128)}, f32[4,64,512]{2,1,0:T(8,128)}) custom-call(s32[1]{0:T(128)S(6)} %copy.12.plan_ref, bf16[128,4096]{1,0:T(8,128)(2,1)} %bitcast.7, bf16[128,512]{1,0:T(8,128)(2,1)} %bitcast.10, bf16[64,512]{1,0:T(8,128)(2,1)} %bitcast.12, ...), custom_call_target="tpu_custom_call" | custom-call | flops 1700000000 | bytes 7340032 | tf_op jit(solution)/shard_map/diloco_step/pallas_call | solution.py:430
  56.9 2.5 %hand_out.1 = (bf16[128,512]{1,0:T(8,128)(2,1)}, bf16[128,4096]{1,0:T(8,128)(2,1)}, bf16[64,512]{1,0:T(8,128)(2,1)}, f32[4,64,512]{2,1,0:T(8,128)}, f32[4,64,512]{2,1,0:T(8,128)}) custom-call(bf16[128,512]{1,0:T(8,128)(2,1)} %get-tuple-element.15.refs_0_, bf16[128,4096]{1,0:T(8,128)(2,1)} %get-tuple-element.16.refs_1_, ...), custom_call_target="tpu_custom_call" | custom-call | tf_op jit(solution)/shard_map/hand_out/pallas_call | solution.py:488

commit v5 on v4

--- a/solution.py
+++ b/solution.py
@@ -358,38 +358,8 @@
 
     zsum[3] = over_b(1, zz)
 
-    for d in ORDER:
-        v_send(d).wait_recv()
-    vout[...] = (vp[rows(a, T)] + vrs[0] + vrs[1] + vrs[2]).astype(BF16)
-    stores.append(pltpu.make_async_copy(vout, values_ref, l_out.at[4]))
-    stores[2].start()
-
-    for k in (0, 1):
-        for h in (0, 1):
-            z_send(k, h).wait_recv()
-    grad = zsum[3] + zrs[0] + zrs[1]
-    inner = wg[1, w_rows(zz)].astype(F32) - RATE * grad
-    picked = jnp.zeros((B, F), F32)
-    for k in range(4):
-        picked = jnp.where(frag == k, gout[k], picked)
-    wout[...] = (0.5 * inner + 0.5 * picked).astype(BF16)
-    stores.append(pltpu.make_async_copy(wout, neww_ref, l_out.at[5]))
-    stores[3].start()
-
-    for half in (0, 1):
-        landed = igrad_ref.at[:, pl.ds(0, 512)]
-        for d in (1, 2, 3):
-            own = ig.at[half, rows((a + d) % 4, T)]
-            back = rdma(own, landed, s_ig.at[half, d - 1], r_ig.at[half, d - 1], at_a(d))
-            back.wait_recv()
-            back.wait_send()
-            for j in range(4):
-                act_send(half, j, d).wait_send()
-        pltpu.make_async_copy(ig.at[half, rows(a, T)], landed, l_out.at[half]).wait()
     for c in cots + wz + wz2 + scatter + spread + [to_core, across]:
         c.wait_send()
-    for d in (1, 2, 3):
-        v_send(d).wait_send()
     for slot in range(4):
         for k in (0, 1):
             wb(slot, k).wait_send()
@@ -402,6 +372,39 @@
     for h in (0, 1):
         for j in range(3):
             b_direct(h, j).wait_send()
+    for half in (0, 1):
+        for d in (1, 2, 3):
+            for j in range(4):
+                act_send(half, j, d).wait_send()
+
+    for d in ORDER:
+        v_send(d).wait_recv()
+    vout[...] = (vp[rows(a, T)] + vrs[0] + vrs[1] + vrs[2]).astype(BF16)
+    stores.append(pltpu.make_async_copy(vout, values_ref, l_out.at[4]))
+    stores[2].start()
+
+    for k in (0, 1):
+        for h in (0, 1):
+            z_send(k, h).wait_recv()
+    grad = zsum[3] + zrs[0] + zrs[1]
+    inner = wg[1, w_rows(zz)].astype(F32) - RATE * grad
+    picked = jnp.zeros((B, F), F32)
+    for k in range(4):
+        picked = jnp.where(frag == k, gout[k], picked)
+    wout[...] = (0.5 * inner + 0.5 * picked).astype(BF16)
+    stores.append(pltpu.make_async_copy(wout, neww_ref, l_out.at[5]))
+    stores[3].start()
+
+    for half in (0, 1):
+        landed = igrad_ref.at[:, pl.ds(0, 512)]
+        for d in (1, 2, 3):
+            own = ig.at[half, rows((a + d) % 4, T)]
+            back = rdma(own, landed, s_ig.at[half, d - 1], r_ig.at[half, d - 1], at_a(d))
+            back.wait_recv()
+            back.wait_send()
+        pltpu.make_async_copy(ig.at[half, rows(a, T)], landed, l_out.at[half]).wait()
+    for d in (1, 2, 3):
+        v_send(d).wait_send()
     for k in (0, 1):
         z_far(k).wait_send()
         for h in (0, 1):

time: 59.6 us -> 59.6 us (level)
  no operation moved by 1% of the time
where the time goes in v5:
time: 59.6 us; the launch traced here: 59.5 us
  Pallas kernels  58.2 us (98%)
  between operations  1.29 us (2%)
    pallas_call x1, Pallas kernels, per_device(): pl.pallas_call(kernel, name='diloco_step', out_shape=(jax.ShapeDtypeStruc...  55.7 us
    pallas_call x1, Pallas kernels, per_device(): pl.pallas_call(hand_out, name='hand_out', out_shape=tuple((jax.ShapeDtype...  2.52 us

profile of v5, /device:TPU:1, one launch (start us, length us, event | category | flops | bytes accessed | tf_op | source)
XLA Modules:
  0.0 59.5 jit_solution(4565352142199665038)
XLA Ops:
  1.3 55.7 %diloco_step.1 = (bf16[128,512]{1,0:T(8,128)(2,1)}, bf16[128,4096]{1,0:T(8,128)(2,1)}, bf16[64,512]{1,0:T(8,128)(2,1)}, f32[4,64,512]{2,1,0:T(8,128)}, f32[4,64,512]{2,1,0:T(8,128)}) custom-call(s32[1]{0:T(128)S(6)} %copy.12.plan_ref, bf16[128,4096]{1,0:T(8,128)(2,1)} %bitcast.7, bf16[128,512]{1,0:T(8,128)(2,1)} %bitcast.10, bf16[64,512]{1,0:T(8,128)(2,1)} %bitcast.12, ...), custom_call_target="tpu_custom_call" | custom-call | flops 1700000000 | bytes 7340032 | tf_op jit(solution)/shard_map/diloco_step/pallas_call | solution.py:433
  56.9 2.5 %hand_out.1 = (bf16[128,512]{1,0:T(8,128)(2,1)}, bf16[128,4096]{1,0:T(8,128)(2,1)}, bf16[64,512]{1,0:T(8,128)(2,1)}, f32[4,64,512]{2,1,0:T(8,128)}, f32[4,64,512]{2,1,0:T(8,128)}) custom-call(bf16[128,512]{1,0:T(8,128)(2,1)} %get-tuple-element.15.refs_0_, bf16[128,4096]{1,0:T(8,128)(2,1)} %get-tuple-element.16.refs_1_, ...), custom_call_target="tpu_custom_call" | custom-call | tf_op jit(solution)/shard_map/hand_out/pallas_call | solution.py:491
